TPU v7x, 128 devices: a whole 4x4x4 slice. The times are simulated.
128 devices in a mesh: rep: 4 (over y_lo, core), gx: 8 (over z, y_hi), gy: 4 (over x).
Axes of the slice: x: 4, y: 4 (y_hi: 2, y_lo: 2; y = y_hi * 2 + y_lo), z: 4, core: 2. Of those that a mesh axis runs over, the one named last changes fastest.
Arguments:
- node_feat: bfloat16 [32768, 256], P(('rep', 'gx', 'gy')), may hold values from -6 to 6
- edge_feat: bfloat16 [1048576, 256], P(('rep', 'gx', 'gy')), may hold values from -6 to 6
- edge_src: int32 [1048576], P(('rep', 'gx', 'gy')), may hold values from 0 to 1023
- edge_dst: int32 [1048576], P(('rep', 'gx', 'gy')), may hold values from 0 to 255
- edge_count: int32 [128], P(('rep', 'gx', 'gy')), may hold values from 2048 to 8192, as said below
- send_idx: int32 [4, 8, 4, 2, 2, 64], P('rep', 'gx', 'gy'), may hold values from 0 to 255
- w_qkv: bfloat16 [2, 256, 768], replicated, may hold values from -0.375 to 0.375
- w_edge: bfloat16 [2, 256, 256], replicated, may hold values from -0.375 to 0.375
- gains: float32 [2, 256], replicated, may hold values from 0.1 to 1.9
- head_in: bfloat16 [256, 256], replicated, may hold values from -0.375 to 0.375
- head_out: bfloat16 [256, 169], replicated, may hold values from -0.375 to 0.375
- targets: bfloat16 [169, 1048576], P(None, ('rep', 'gx', 'gy')), may hold values from -15 to 15
Outputs:
- node_out: bfloat16 [32768, 256], P(('rep', 'gx', 'gy'))
- grad_head_in: float32 [256, 256], replicated
- grad_head_out: float32 [256, 169], replicated
Inputs may be any that keep to these rules, and one draw needn't show every extreme that they name: `edge_count`: edge slots of a tile at positions from its count on are padding; some tile holds 8192 live edges.
All inputs are finite; a program needn't handle non-finite values.
Results may differ from a plain program's by a relative error of at most 0.0025.
The roundings to bfloat16 on the way count: a program that leaves them out, or rounds other values in their place, can miss the bound.
Values may be sent and summed in bfloat16 or wider, within the bound.
No kernel may reach another device: no remote copies, remote signals or barrier semaphores. Data moves between devices by JAX's collectives and lax.ppermute only.
A program may use at most 128 MiB of HBM per device.

v0:
```python
import math
import jax
import jax.numpy as jnp
from jax import lax
from jax.sharding import PartitionSpec as P

OUTER_CELLS = (
    (0, 0),
    (0, 1),
    (0, 2),
    (0, 3),
    (1, 0),
    (1, 3),
    (2, 0),
    (2, 3),
    (3, 0),
    (3, 1),
    (3, 2),
    (3, 3),
)


def with_halo(x, sides, width):
    for axis, dim in sides:
        count, length = (lax.axis_size(axis), x.shape[dim])
        up = [(i, (i + 1) % count) for i in range(count)]
        down = [(j, i) for i, j in up]
        last = lax.slice_in_dim(x, length - width, length, axis=dim)
        initial = lax.slice_in_dim(x, 0, width, axis=dim)
        before = lax.ppermute(last, axis, up)
        after = lax.ppermute(initial, axis, down)
        x = jnp.concatenate([before, x, after], axis=dim)
    return x


def layer_norm(values):
    centre = values - jnp.mean(values, axis=-1, keepdims=True)
    spread = jnp.mean(centre * centre, axis=-1, keepdims=True)
    return centre * lax.rsqrt(spread + 1e-05)


def outer_rows(padded):
    return jnp.concatenate([padded[cell_i, cell_j] for cell_i, cell_j in OUTER_CELLS], axis=0)


def edge_pass(table, query_part, edges, edge_src, edge_dst, live_column, weight_edge):
    edge_slots, feature_width = edges.shape
    atom_count = query_part.shape[0]
    table_rows = table.shape[0]
    block_rows = math.gcd(edge_slots, 2048)
    block_count = edge_slots // block_rows
    table_iota = jnp.arange(table_rows, dtype=jnp.int32)
    atom_iota = jnp.arange(atom_count, dtype=jnp.int32)

    def one_block(carry, items):
        edge_rows, source_rows, target_rows, live_rows = items
        source_hot = (source_rows[:, None] == table_iota[None, :]).astype(jnp.bfloat16)
        target_hot = (target_rows[:, None] == atom_iota[None, :]).astype(jnp.bfloat16)
        gathered = jnp.dot(source_hot, table, preferred_element_type=jnp.float32)
        queries = jnp.dot(target_hot, query_part, preferred_element_type=jnp.float32)
        pre_act = queries + gathered[:, :feature_width]
        pre_act = pre_act + jnp.dot(edge_rows, weight_edge, preferred_element_type=jnp.float32)
        new_rows = (edge_rows.astype(jnp.float32) + live_rows * jax.nn.silu(pre_act)).astype(
            jnp.bfloat16
        )
        weighted = live_rows * jax.nn.sigmoid(pre_act) * gathered[:, feature_width:]
        added = lax.dot_general(
            target_hot.astype(jnp.float32),
            weighted,
            (((0,), (0,)), ((), ())),
            precision=lax.Precision.HIGHEST,
            preferred_element_type=jnp.float32,
        )
        return (carry + added, new_rows)

    start = jnp.zeros((atom_count, feature_width), jnp.float32)
    items = (
        edges.reshape(block_count, block_rows, feature_width),
        edge_src.reshape(block_count, block_rows),
        edge_dst.reshape(block_count, block_rows),
        live_column.reshape(block_count, block_rows, 1),
    )
    summed, new_blocks = lax.scan(one_block, start, items)
    return (summed, new_blocks.reshape(edge_slots, feature_width))


def body(
    node_feat,
    edge_feat,
    edge_src,
    edge_dst,
    edge_count,
    send_idx,
    w_qkv,
    w_edge,
    gains,
    head_in,
    head_out,
    targets,
):
    feature_width = node_feat.shape[1]
    edge_slots = edge_feat.shape[0]
    cell_rows = send_idx.shape[-1]
    corner_index = send_idx.reshape(2, 2, cell_rows)
    positions = jnp.arange(edge_slots, dtype=jnp.int32)
    live_column = (positions < edge_count[0]).astype(jnp.float32)[:, None]
    nodes = node_feat
    edges = edge_feat
    for layer_index in range(w_qkv.shape[0]):
        weight_qkv = w_qkv[layer_index]
        projected = jnp.dot(nodes, weight_qkv, preferred_element_type=jnp.float32).astype(
            jnp.bfloat16
        )
        local_kv = projected[:, feature_width:]
        padded = with_halo(nodes[corner_index], (("gx", 0), ("gy", 1)), 1)
        ghost_kv = jnp.dot(
            outer_rows(padded), weight_qkv[:, feature_width:], preferred_element_type=jnp.float32
        ).astype(jnp.bfloat16)
        table = jnp.concatenate([local_kv, ghost_kv], axis=0)
        summed, edges = edge_pass(
            table,
            projected[:, :feature_width],
            edges,
            edge_src,
            edge_dst,
            live_column,
            w_edge[layer_index],
        )
        nodes = (nodes.astype(jnp.float32) + gains[layer_index] * layer_norm(summed)).astype(
            jnp.bfloat16
        )
    scale = 0.125 / (edge_slots * lax.axis_size(("rep", "gx", "gy"))) ** 0.5
    act_in = jnp.dot(edges, head_in, preferred_element_type=jnp.float32)
    hidden_head = jax.nn.silu(act_in).astype(jnp.bfloat16)
    pred = lax.dot_general(
        head_out, hidden_head, (((0,), (1,)), ((), ())), preferred_element_type=jnp.float32
    )
    live_row = live_column[:, 0][None, :]
    dpred = (live_row * (pred - targets.astype(jnp.float32)) * scale).astype(jnp.bfloat16)
    dhidden = lax.dot_general(
        dpred, head_out, (((0,), (1,)), ((), ())), preferred_element_type=jnp.float32
    )
    sigmoid_in = jax.nn.sigmoid(act_in)
    dact = (dhidden * sigmoid_in * (1.0 + act_in * (1.0 - sigmoid_in))).astype(jnp.bfloat16)
    grad_in = lax.dot_general(
        edges, dact, (((0,), (0,)), ((), ())), preferred_element_type=jnp.float32
    )
    grad_out = lax.dot_general(
        hidden_head, dpred, (((0,), (1,)), ((), ())), preferred_element_type=jnp.float32
    )
    grad_in, grad_out = lax.psum((grad_in, grad_out), ("rep", "gx", "gy"))
    return (nodes, grad_in, grad_out)


def solution(mesh):
    return jax.shard_map(
        body,
        mesh=mesh,
        in_specs=(
            P(("rep", "gx", "gy"), None),
            P(("rep", "gx", "gy"), None),
            P(("rep", "gx", "gy")),
            P(("rep", "gx", "gy")),
            P(("rep", "gx", "gy")),
            P("rep", "gx", "gy", None, None, None),
            P(),
            P(),
            P(),
            P(),
            P(),
            P(None, ("rep", "gx", "gy")),
        ),
        out_specs=(P(("rep", "gx", "gy"), None), P(), P()),
        check_vma=False,
    )
```

profile of v0, /device:TPU:1, one launch (start us, length us, event | category | flops | bytes accessed | tf_op | source)
XLA Modules:
  0.0 348.6 jit_solution(3398888422495279461)
XLA Ops:
  10.1 3.8 %collective-permute-start = (bf16[1,2,64,256]{3,2,1,0:T(8,128)(2,1)S(1)}, bf16[1,2,64,256]{3,2,1,0:T(8,128)(2,1)S(1)}, u32[]{:S(2)}, u32[]{:S(2)}) collective-permute-start(bf16[1,2,64,256]{3,2,1,0:T(8,128)(2,1)S(1)} %bitcast.229), channel_id=1, source_target_pairs={{0,4},{4,8},{8,12},{12,16},{16,20},{20,24},{24,28},{28,0},{1,5},{5... | collective-permute-start | bytes 196616 | tf_op jit(solution)/shard_map/ppermute | solution.py:30
  13.9 3.6 %collective-permute-start.1 = (bf16[1,2,64,256]{3,2,1,0:T(8,128)(2,1)S(1)}, bf16[1,2,64,256]{3,2,1,0:T(8,128)(2,1)S(1)}, u32[]{:S(2)}, u32[]{:S(2)}) collective-permute-start(bf16[1,2,64,256]{3,2,1,0:T(8,128)(2,1)S(1)} %bitcast.228), channel_id=1, source_target_pairs={{4,0},{8,4},{12,8},{16,12},{20,16},{24,20},{28,24},{0,28},{5,1},{9... | collective-permute-start | bytes 196616 | tf_op jit(solution)/shard_map/ppermute | solution.py:31
  34.5 61.8 %while.26 = (s32[]{:T(128)}, f32[256,256]{1,0:T(8,128)S(1)}, bf16[4,2048,256]{2,1,0:T(8,128)(2,1)}, s32[4,2048]{1,0:T(4,128)S(1)}, f32[4,2048,1]{1,2,0:T(1,128)S...) while((s32[]{:T(128)}, f32[256,256]{1,0:T(8,128)S(1)}, ...), condition=%wide.region_1.2_spmd.clone, body=%wide.region_0.1_spmd.clone.sunk | while | flops 4306108416 | bytes 55403708 | solution.py:83
  34.6 3.6 %fusion.83 = f32[2048,512]{1,0:T(8,128)S(1)} fusion(bf16[1024,512]{1,0:T(8,128)(2,1)} %get-tuple-element.442, s32[2048]{0:T(1024)S(1)} %bitcast.226), kind=kOutput, calls=%fused_computation.7.clone.1 | convolution fusion | flops 2149580800 | bytes 5251072 | tf_op jit(solution)/shard_map/while/body/eval_jaxpr/dot_general | solution.py:59
  41.9 2.6 bitcast_dynamic-update-slice_fusion.4
  44.6 5.5 %fusion.84 = f32[256,256]{1,0:T(8,128)S(1)} fusion(f32[2048,512]{1,0:T(8,128)} %copy-done.1, f32[2048,256]{1,0:T(8,128)} %get-tuple-element.395, f32[2048]{0:T(1024)S(1)} %bitcast.223, s32[2048]{0:T(1024)S(1)} %bitcast.219, f32[256,256]{1,0:T(8,128)S(1)} %get-tuple-element.424, pred[]{:T(512)S(6)} %compare.6), kind=kOutput, calls=%fused_computation.17.clone.1 | convolution fusion | flops 1613889536 | bytes 4734977 | tf_op jit(solution)/shard_map/while/body/eval_jaxpr/dot_general | solution.py:67
  50.1 3.6 %fusion.83 = f32[2048,512]{1,0:T(8,128)S(1)} fusion(bf16[1024,512]{1,0:T(8,128)(2,1)} %get-tuple-element.442, s32[2048]{0:T(1024)S(1)} %bitcast.226), kind=kOutput, calls=%fused_computation.7.clone.1 | convolution fusion | flops 2149580800 | bytes 5251072 | tf_op jit(solution)/shard_map/while/body/eval_jaxpr/dot_general | solution.py:59
  60.0 5.5 %fusion.84 = f32[256,256]{1,0:T(8,128)S(1)} fusion(f32[2048,512]{1,0:T(8,128)} %copy-done.1, f32[2048,256]{1,0:T(8,128)} %get-tuple-element.395, f32[2048]{0:T(1024)S(1)} %bitcast.223, s32[2048]{0:T(1024)S(1)} %bitcast.219, f32[256,256]{1,0:T(8,128)S(1)} %get-tuple-element.424, pred[]{:T(512)S(6)} %compare.6), kind=kOutput, calls=%fused_computation.17.clone.1 | convolution fusion | flops 1613889536 | bytes 4734977 | tf_op jit(solution)/shard_map/while/body/eval_jaxpr/dot_general | solution.py:67
  65.5 3.6 %fusion.83 = f32[2048,512]{1,0:T(8,128)S(1)} fusion(bf16[1024,512]{1,0:T(8,128)(2,1)} %get-tuple-element.442, s32[2048]{0:T(1024)S(1)} %bitcast.226), kind=kOutput, calls=%fused_computation.7.clone.1 | convolution fusion | flops 2149580800 | bytes 5251072 | tf_op jit(solution)/shard_map/while/body/eval_jaxpr/dot_general | solution.py:59
  75.4 5.5 %fusion.84 = f32[256,256]{1,0:T(8,128)S(1)} fusion(f32[2048,512]{1,0:T(8,128)} %copy-done.1, f32[2048,256]{1,0:T(8,128)} %get-tuple-element.395, f32[2048]{0:T(1024)S(1)} %bitcast.223, s32[2048]{0:T(1024)S(1)} %bitcast.219, f32[256,256]{1,0:T(8,128)S(1)} %get-tuple-element.424, pred[]{:T(512)S(6)} %compare.6), kind=kOutput, calls=%fused_computation.17.clone.1 | convolution fusion | flops 1613889536 | bytes 4734977 | tf_op jit(solution)/shard_map/while/body/eval_jaxpr/dot_general | solution.py:67
  80.9 3.6 %fusion.83 = f32[2048,512]{1,0:T(8,128)S(1)} fusion(bf16[1024,512]{1,0:T(8,128)(2,1)} %get-tuple-element.442, s32[2048]{0:T(1024)S(1)} %bitcast.226), kind=kOutput, calls=%fused_computation.7.clone.1 | convolution fusion | flops 2149580800 | bytes 5251072 | tf_op jit(solution)/shard_map/while/body/eval_jaxpr/dot_general | solution.py:59
  88.3 2.6 bitcast_dynamic-update-slice_fusion.4
  90.9 5.5 %fusion.84 = f32[256,256]{1,0:T(8,128)S(1)} fusion(f32[2048,512]{1,0:T(8,128)} %copy-done.1, f32[2048,256]{1,0:T(8,128)} %get-tuple-element.395, f32[2048]{0:T(1024)S(1)} %bitcast.223, s32[2048]{0:T(1024)S(1)} %bitcast.219, f32[256,256]{1,0:T(8,128)S(1)} %get-tuple-element.424, pred[]{:T(512)S(6)} %compare.6), kind=kOutput, calls=%fused_computation.17.clone.1 | convolution fusion | flops 1613889536 | bytes 4734977 | tf_op jit(solution)/shard_map/while/body/eval_jaxpr/dot_general | solution.py:67
  98.3 4.8 %collective-permute-start.5 = (bf16[1,2,64,256]{3,2,1,0:T(8,128)(2,1)S(1)}, bf16[1,2,64,256]{3,2,1,0:T(8,128)(2,1)S(1)}, u32[]{:S(2)}, u32[]{:S(2)}) collective-permute-start(bf16[1,2,64,256]{3,2,1,0:T(8,128)(2,1)S(1)} %bitcast.230), channel_id=1, source_target_pairs={{4,0},{8,4},{12,8},{16,12},{20,16},{24,20},{28,24},{0,28},{5,1},{9... | collective-permute-start | bytes 196616 | tf_op jit(solution)/shard_map/ppermute | solution.py:31
  105.5 2.7 collective-permute-start.7
  113.0 56.8 %while.27 = (s32[]{:T(128)}, f32[256,256]{1,0:T(8,128)S(1)}, bf16[4,2048,256]{2,1,0:T(8,128)(2,1)}, s32[4,2048]{1,0:T(4,128)S(1)}, f32[4,2048,1]{1,2,0:T(1,128)S...) while((s32[]{:T(128)}, f32[256,256]{1,0:T(8,128)S(1)}, ...), condition=%wide.region_5.6_spmd.clone, body=%wide.region_4.5_spmd.clone.sunk | while | flops 4306108416 | bytes 55403708 | solution.py:83
  119.1 2.6 bitcast_dynamic-update-slice_fusion.5
  121.7 5.5 %fusion.89 = f32[256,256]{1,0:T(8,128)S(1)} fusion(f32[2048,512]{1,0:T(8,128)} %copy-done.2, f32[2048,256]{1,0:T(8,128)} %get-tuple-element.409, f32[2048]{0:T(1024)S(1)} %bitcast.225, s32[2048]{0:T(1024)S(1)} %bitcast.221, f32[256,256]{1,0:T(8,128)S(1)} %get-tuple-element.460, pred[]{:T(512)S(6)} %compare.7), kind=kOutput, calls=%fused_computation.41.clone.1 | convolution fusion | flops 1613889536 | bytes 4734977 | tf_op jit(solution)/shard_map/while/body/eval_jaxpr/dot_general | solution.py:67
  135.9 5.5 %fusion.89 = f32[256,256]{1,0:T(8,128)S(1)} fusion(f32[2048,512]{1,0:T(8,128)} %copy-done.2, f32[2048,256]{1,0:T(8,128)} %get-tuple-element.409, f32[2048]{0:T(1024)S(1)} %bitcast.225, s32[2048]{0:T(1024)S(1)} %bitcast.221, f32[256,256]{1,0:T(8,128)S(1)} %get-tuple-element.460, pred[]{:T(512)S(6)} %compare.7), kind=kOutput, calls=%fused_computation.41.clone.1 | convolution fusion | flops 1613889536 | bytes 4734977 | tf_op jit(solution)/shard_map/while/body/eval_jaxpr/dot_general | solution.py:67
  150.1 5.5 %fusion.89 = f32[256,256]{1,0:T(8,128)S(1)} fusion(f32[2048,512]{1,0:T(8,128)} %copy-done.2, f32[2048,256]{1,0:T(8,128)} %get-tuple-element.409, f32[2048]{0:T(1024)S(1)} %bitcast.225, s32[2048]{0:T(1024)S(1)} %bitcast.221, f32[256,256]{1,0:T(8,128)S(1)} %get-tuple-element.460, pred[]{:T(512)S(6)} %compare.7), kind=kOutput, calls=%fused_computation.41.clone.1 | convolution fusion | flops 1613889536 | bytes 4734977 | tf_op jit(solution)/shard_map/while/body/eval_jaxpr/dot_general | solution.py:67
  164.3 5.5 %fusion.89 = f32[256,256]{1,0:T(8,128)S(1)} fusion(f32[2048,512]{1,0:T(8,128)} %copy-done.2, f32[2048,256]{1,0:T(8,128)} %get-tuple-element.409, f32[2048]{0:T(1024)S(1)} %bitcast.225, s32[2048]{0:T(1024)S(1)} %bitcast.221, f32[256,256]{1,0:T(8,128)S(1)} %get-tuple-element.460, pred[]{:T(512)S(6)} %compare.7), kind=kOutput, calls=%fused_computation.41.clone.1 | convolution fusion | flops 1613889536 | bytes 4734977 | tf_op jit(solution)/shard_map/while/body/eval_jaxpr/dot_general | solution.py:67
  169.8 6.9 %multiply_convert_fusion = (bf16[8192,256]{1,0:T(8,128)(2,1)S(1)}, f32[8192,256]{1,0:T(8,128)}) fusion(bf16[8192,256]{1,0:T(8,128)(2,1)} %bitcast.214, bf16[256,256]{1,0:T(8,128)(2,1)S(1)} %copy-done), kind=kOutput, calls=%fused_computation.62 | convolution fusion | flops 1084227584 | bytes 16908288 | tf_op jit(solution)/shard_map/dot_general | solution.py:133
  179.9 9.2 %fusion.40 = f32[256,256]{1,0:T(8,128)} fusion(bf16[8192,256]{1,0:T(8,128)(2,1)} %bitcast.215, bf16[169,8192]{1,0:T(8,128)(2,1)S(1)} %fusion.39, bf16[256,169]{0,1:T(8,128)(2,1)S(1)} %copy-done.18, f32[8192,256]{1,0:T(8,128)} %get-tuple-element.272), kind=kOutput, calls=%fused_computation.64 | convolution fusion | flops 1801453568 | bytes 15700480 | tf_op jit(solution)/shard_map/dot_general | solution.py:145
  190.3 148.2 %all-reduce.3.cloned.1.call-done = (f32[256,256]{1,0:T(8,128)}, f32[256,169]{0,1:T(8,128)}) async-done(((f32[256,256]{1,0:T(8,128)}, f32[256,169]{0,1:T(8,128)}), (f32[256,256]{1,0:T(8,128)}, f32[256,169]{0,1:T(8,128)})) %all-reduce.3.cloned.1.call-update) | async-done | bytes 435216 | tf_op jit(solution)/shard_map/psum | solution.py:151
  (180 shorter events, 87.6 us)
Async XLA Ops:
  7.2 162.6 %copy-start = (bf16[256,256]{1,0:T(8,128)(2,1)S(1)}, bf16[256,256]{1,0:T(8,128)(2,1)}, u32[]{:S(2)}) copy-start(bf16[256,256]{1,0:T(8,128)(2,1)} %param.25) | copy-start | bytes 393220
  7.2 11.4 %copy-start.3 = (bf16[256,256]{1,0:T(8,128)(2,1)S(1)}, bf16[256,256]{1,0:T(8,128)(2,1)}, u32[]{:S(2)}) copy-start(bf16[256,256]{1,0:T(8,128)(2,1)} %param.16) | copy-start | bytes 393220
  7.2 11.4 %copy-start.6 = (bf16[2,256,768]{2,1,0:T(8,128)(2,1)S(1)}, bf16[2,256,768]{2,1,0:T(8,128)(2,1)}, u32[]{:S(2)}) copy-start(bf16[2,256,768]{2,1,0:T(8,128)(2,1)} %param.22) | copy-start | bytes 2359300
  7.2 12.4 %copy-start.7 = (bf16[2,256,256]{2,1,0:T(8,128)(2,1)S(1)}, bf16[2,256,256]{2,1,0:T(8,128)(2,1)}, u32[]{:S(2)}) copy-start(bf16[2,256,256]{2,1,0:T(8,128)(2,1)} %param.23) | copy-start | bytes 786436
  7.2 13.2 %copy-start.12 = (s32[8192]{0:T(1024)S(1)}, s32[8192]{0:T(1024)}, u32[]{:S(2)}) copy-start(s32[8192]{0:T(1024)} %param.19) | copy-start | bytes 98308
  7.2 13.2 %copy-start.13 = (s32[8192]{0:T(1024)S(1)}, s32[8192]{0:T(1024)}, u32[]{:S(2)}) copy-start(s32[8192]{0:T(1024)} %param.18) | copy-start | bytes 98308
  7.2 331.3 %all-reduce.3.cloned.1.call-start = ((), (), s32[]{:S(2)}) async-start(), calls=%async_computation | async-start | bytes 884736 | tf_op jit(solution)/shard_map/psum | solution.py:151
  10.0 13.9 %copy-start.15 = (f32[2,256]{1,0:T(2,128)S(1)}, f32[2,256]{1,0:T(2,128)}, u32[]{:S(2)}) copy-start(f32[2,256]{1,0:T(2,128)} %param.24) | copy-start | bytes 6148
  10.1 10.4 %collective-permute-start = (bf16[1,2,64,256]{3,2,1,0:T(8,128)(2,1)S(1)}, bf16[1,2,64,256]{3,2,1,0:T(8,128)(2,1)S(1)}, u32[]{:S(2)}, u32[]{:S(2)}) collective-permute-start(bf16[1,2,64,256]{3,2,1,0:T(8,128)(2,1)S(1)} %bitcast.229), channel_id=1, source_target_pairs={{0,4},{4,8},{8,12},{12,16},{16,20},{20,24},{24,28},{28,0},{1,5},{5... | collective-permute-start | bytes 196616 | tf_op jit(solution)/shard_map/ppermute | solution.py:30
  13.9 6.6 %collective-permute-start.1 = (bf16[1,2,64,256]{3,2,1,0:T(8,128)(2,1)S(1)}, bf16[1,2,64,256]{3,2,1,0:T(8,128)(2,1)S(1)}, u32[]{:S(2)}, u32[]{:S(2)}) collective-permute-start(bf16[1,2,64,256]{3,2,1,0:T(8,128)(2,1)S(1)} %bitcast.228), channel_id=1, source_target_pairs={{4,0},{8,4},{12,8},{16,12},{20,16},{24,20},{28,24},{0,28},{5,1},{9... | collective-permute-start | bytes 196616 | tf_op jit(solution)/shard_map/ppermute | solution.py:31
  18.9 13.4 %copy-start.4 = (bf16[256,768]{1,0:T(8,128)(2,1)}, bf16[256,768]{1,0:T(8,128)(2,1)S(1)}, u32[]{:S(2)}) copy-start(bf16[256,768]{1,0:T(8,128)(2,1)S(1)} %convolution_convert_fusion.3) | copy-start | bytes 1179652
  22.6 5.1 %collective-permute-start.2 = (bf16[4,1,64,256]{3,2,1,0:T(8,128)(2,1)S(1)}, bf16[4,1,64,256]{3,2,1,0:T(8,128)(2,1)S(1)}, u32[]{:S(2)}, u32[]{:S(2)}) collective-permute-start(bf16[4,1,64,256]{3,2,1,0:T(8,128)(2,1)S(1)} %get-tuple-element.264), channel_id=1, source_target_pairs={{0,1},{1,2},{2,3},{3,0},{4,5},{5,6},{6,7},{7,4},{8,9},{9,10},{10,1... | collective-permute-start | bytes 393224 | tf_op jit(solution)/shard_map/ppermute | solution.py:30
  24.5 4.8 %collective-permute-start.3 = (bf16[4,1,64,256]{3,2,1,0:T(8,128)(2,1)S(1)}, bf16[4,1,64,256]{3,2,1,0:T(8,128)(2,1)S(1)}, u32[]{:S(2)}, u32[]{:S(2)}) collective-permute-start(bf16[4,1,64,256]{3,2,1,0:T(8,128)(2,1)S(1)} %get-tuple-element.263), channel_id=1, source_target_pairs={{1,0},{2,1},{3,2},{0,3},{5,4},{6,5},{7,6},{4,7},{9,8},{10,9},{11,1... | collective-permute-start | bytes 393224 | tf_op jit(solution)/shard_map/ppermute | solution.py:31
  38.2 6.4 %copy-start.1 = (f32[2048,512]{1,0:T(8,128)}, f32[2048,512]{1,0:T(8,128)S(1)}, u32[]{:S(2)}) copy-start(f32[2048,512]{1,0:T(8,128)S(1)} %fusion.83) | copy-start | bytes 12582916 | tf_op jit(solution)/shard_map/while
  84.5 6.3 %copy-start.1 = (f32[2048,512]{1,0:T(8,128)}, f32[2048,512]{1,0:T(8,128)S(1)}, u32[]{:S(2)}) copy-start(f32[2048,512]{1,0:T(8,128)S(1)} %fusion.83) | copy-start | bytes 12582916 | tf_op jit(solution)/shard_map/while
  98.0 6.8 %collective-permute-start.4 = (bf16[1,2,64,256]{3,2,1,0:T(8,128)(2,1)S(1)}, bf16[1,2,64,256]{3,2,1,0:T(8,128)(2,1)S(1)}, u32[]{:S(2)}, u32[]{:S(2)}) collective-permute-start(bf16[1,2,64,256]{3,2,1,0:T(8,128)(2,1)S(1)} %bitcast.231), channel_id=1, source_target_pairs={{0,4},{4,8},{8,12},{12,16},{16,20},{20,24},{24,28},{28,0},{1,5},{5... | collective-permute-start | bytes 196616 | tf_op jit(solution)/shard_map/ppermute | solution.py:30
  98.3 6.5 %collective-permute-start.5 = (bf16[1,2,64,256]{3,2,1,0:T(8,128)(2,1)S(1)}, bf16[1,2,64,256]{3,2,1,0:T(8,128)(2,1)S(1)}, u32[]{:S(2)}, u32[]{:S(2)}) collective-permute-start(bf16[1,2,64,256]{3,2,1,0:T(8,128)(2,1)S(1)} %bitcast.230), channel_id=1, source_target_pairs={{4,0},{8,4},{12,8},{16,12},{20,16},{24,20},{28,24},{0,28},{5,1},{9... | collective-permute-start | bytes 196616 | tf_op jit(solution)/shard_map/ppermute | solution.py:31
  104.9 5.1 %collective-permute-start.6 = (bf16[4,1,64,256]{3,2,1,0:T(8,128)(2,1)S(1)}, bf16[4,1,64,256]{3,2,1,0:T(8,128)(2,1)S(1)}, u32[]{:S(2)}, u32[]{:S(2)}) collective-permute-start(bf16[4,1,64,256]{3,2,1,0:T(8,128)(2,1)S(1)} %get-tuple-element.262), channel_id=1, source_target_pairs={{0,1},{1,2},{2,3},{3,0},{4,5},{5,6},{6,7},{7,4},{8,9},{9,10},{10,1... | collective-permute-start | bytes 393224 | tf_op jit(solution)/shard_map/ppermute | solution.py:30
  105.5 4.7 %collective-permute-start.7 = (bf16[4,1,64,256]{3,2,1,0:T(8,128)(2,1)S(1)}, bf16[4,1,64,256]{3,2,1,0:T(8,128)(2,1)S(1)}, u32[]{:S(2)}, u32[]{:S(2)}) collective-permute-start(bf16[4,1,64,256]{3,2,1,0:T(8,128)(2,1)S(1)} %get-tuple-element.261), channel_id=1, source_target_pairs={{1,0},{2,1},{3,2},{0,3},{5,4},{6,5},{7,6},{4,7},{9,8},{10,9},{11,1... | collective-permute-start | bytes 393224 | tf_op jit(solution)/shard_map/ppermute | solution.py:31
  115.4 6.3 %copy-start.2 = (f32[2048,512]{1,0:T(8,128)}, f32[2048,512]{1,0:T(8,128)S(1)}, u32[]{:S(2)}) copy-start(f32[2048,512]{1,0:T(8,128)S(1)} %fusion.88) | copy-start | bytes 12582916 | tf_op jit(solution)/shard_map/while
  143.8 6.3 %copy-start.2 = (f32[2048,512]{1,0:T(8,128)}, f32[2048,512]{1,0:T(8,128)S(1)}, u32[]{:S(2)}) copy-start(f32[2048,512]{1,0:T(8,128)S(1)} %fusion.88) | copy-start | bytes 12582916 | tf_op jit(solution)/shard_map/while
  169.8 6.9 %copy-start.17 = (bf16[169,8192]{1,0:T(8,128)(2,1)S(1)}, bf16[169,8192]{1,0:T(8,128)(2,1)}, u32[]{:S(2)}) copy-start(bf16[169,8192]{1,0:T(8,128)(2,1)} %param.27) | copy-start | bytes 8306692
  169.8 6.9 %copy-start.18 = (bf16[256,169]{0,1:T(8,128)(2,1)S(1)}, bf16[256,169]{0,1:T(8,128)(2,1)}, u32[]{:S(2)}) copy-start(bf16[256,169]{0,1:T(8,128)(2,1)} %param.26) | copy-start | bytes 259588
  179.9 9.6 %copy-start.14 = (f32[1,256]{1,0:T(1,128)S(1)}, f32[1,256]{1,0:T(1,128)}, u32[]{:S(2)}) copy-start(f32[1,256]{1,0:T(1,128)} %get-tuple-element.269) | copy-start | bytes 3076
  (17 other events, 63.9 us)
Sparse Core Ops, SparseCore 0:
  189.6 148.8 all-reduce.2
where the time goes:
time: 350 us; the launch traced here: 349 us
  waiting for transfers between devices  154 us (44%)
  matrix products  122 us (35%)
  local copies, waits for them, and re-layouts  34.6 us (10%)
  starting transfers between devices  18.3 us (5%)
  between operations  15.2 us (4%)
  other arithmetic  4.44 us (1%)
    psum x1, waiting for transfers between devices, body(): grad_in, grad_out = lax.psum((grad_in, grad_out), ('rep', 'gx', 'gy'))  148 us
    dot_general x8, matrix products, one_block(): lax.dot_general(target_hot.astype(jnp.float32), weighted, (((0,), (0,)),...  43.6 us
    dot_general x8, matrix products, one_block(): gathered = jnp.dot(source_hot, table, preferred_element_type=jnp.float32)  24.1 us
    dot_general x8, matrix products, one_block(): jnp.dot(edge_rows, weight_edge, preferred_element_type=jnp.float32)  20.7 us
    while x32, local copies, waits for them, and re-layouts  16.4 us
    dot_general x8, matrix products, one_block(): jnp.dot(target_hot, query_part, preferred_element_type=jnp.float32)  13 us
    ppermute x4, starting transfers between devices, with_halo(): after = lax.ppermute(initial, axis, down)  12.6 us
    dot_general x1, matrix products, body(): lax.dot_general(edges, dact, (((0,), (0,)), ((), ())), preferred_element_...  9.24 us
  transfers between devices with their start and end apart: 9, of which 5 were waited for; matrix products, arithmetic and copies ran while one was open for 2% of the time, Pallas kernels for 0%

commit v1 on v0

--- a/solution.py
+++ b/solution.py
@@ -18,6 +18,12 @@
     (3, 2),
     (3, 3),
 )
+
+
+def begin_the_things(axis_name, axis_id, x_local):
+    for u in (axis_name, axis_id):
+        x_local = lax.psum(x_local, u)
+    return x_local
 
 
 def with_halo(x, sides, width):
@@ -148,7 +154,7 @@
     grad_out = lax.dot_general(
         hidden_head, dpred, (((0,), (1,)), ((), ())), preferred_element_type=jnp.float32
     )
-    grad_in, grad_out = lax.psum((grad_in, grad_out), ("rep", "gx", "gy"))
+    grad_in, grad_out = begin_the_things("rep", ("gx", "gy"), (grad_in, grad_out))
     return (nodes, grad_in, grad_out)
 
 

time: 350 us -> 588 us (1.68)
  the two profiles are of different devices: /device:TPU:1 before, /device:TPU:2 now
where the time goes in v1:
time: 588 us; the launch traced here: 587 us
  waiting for transfers between devices  393 us (67%)
  matrix products  122 us (21%)
  local copies, waits for them, and re-layouts  34.6 us (6%)
  starting transfers between devices  16.9 us (3%)
  between operations  15.2 us (3%)
    psum x2, waiting for transfers between devices, begin_the_things(): x_local = lax.psum(x_local, u)  384 us
    dot_general x8, matrix products, one_block(): lax.dot_general(target_hot.astype(jnp.float32), weighted, (((0,), (0,)),...  43.7 us
    dot_general x8, matrix products, one_block(): gathered = jnp.dot(source_hot, table, preferred_element_type=jnp.float32)  24.1 us
    dot_general x8, matrix products, one_block(): jnp.dot(edge_rows, weight_edge, preferred_element_type=jnp.float32)  20.7 us
    while x32, local copies, waits for them, and re-layouts  16.4 us
    dot_general x8, matrix products, one_block(): jnp.dot(target_hot, query_part, preferred_element_type=jnp.float32)  13 us
  transfers between devices with their start and end apart: 10, of which 7 were waited for; matrix products, arithmetic and copies ran while one was open for 1% of the time, Pallas kernels for 0%

profile of v1, /device:TPU:2, one launch (start us, length us, event | category | flops | bytes accessed | tf_op | source)
XLA Modules:
  0.0 586.8 jit_solution(14415260752648051621)
XLA Ops:
  10.1 3.3 collective-permute-start
  13.3 3.6 collective-permute-start.1
  34.5 61.8 %while.26 = (s32[]{:T(128)}, f32[256,256]{1,0:T(8,128)S(1)}, bf16[4,2048,256]{2,1,0:T(8,128)(2,1)}, s32[4,2048]{1,0:T(4,128)S(1)}, f32[4,2048,1]{1,2,0:T(1,128)S...) while((s32[]{:T(128)}, f32[256,256]{1,0:T(8,128)S(1)}, ...), condition=%wide.region_1.2_spmd.clone, body=%wide.region_0.1_spmd.clone.sunk | while | flops 4306108416 | bytes 55403708 | solution.py:89
  34.5 3.6 fusion.83
  41.8 2.6 bitcast_dynamic-update-slice_fusion.4
  44.5 5.5 fusion.84
  50.0 3.6 fusion.83
  59.9 5.5 fusion.84
  65.4 3.6 fusion.83
  75.3 5.5 fusion.84
  80.8 3.6 fusion.83
  88.2 2.6 bitcast_dynamic-update-slice_fusion.4
  90.8 5.5 fusion.84
  99.2 4.5 collective-permute-start.5
  115.4 56.8 %while.27 = (s32[]{:T(128)}, f32[256,256]{1,0:T(8,128)S(1)}, bf16[4,2048,256]{2,1,0:T(8,128)(2,1)}, s32[4,2048]{1,0:T(4,128)S(1)}, f32[4,2048,1]{1,2,0:T(1,128)S...) while((s32[]{:T(128)}, f32[256,256]{1,0:T(8,128)S(1)}, ...), condition=%wide.region_5.6_spmd.clone, body=%wide.region_4.5_spmd.clone.sunk | while | flops 4306108416 | bytes 55403708 | solution.py:89
  121.6 2.6 bitcast_dynamic-update-slice_fusion.5
  124.2 5.5 fusion.89
  138.3 5.5 fusion.89
  152.5 5.5 fusion.89
  166.7 5.5 fusion.89
  172.2 6.9 %multiply_convert_fusion = (bf16[8192,256]{1,0:T(8,128)(2,1)S(1)}, f32[8192,256]{1,0:T(8,128)}) fusion(bf16[8192,256]{1,0:T(8,128)(2,1)} %bitcast.214, bf16[256,256]{1,0:T(8,128)(2,1)S(1)} %copy-done), kind=kOutput, calls=%fused_computation.62 | convolution fusion | flops 1084227584 | bytes 16908288 | tf_op jit(solution)/shard_map/dot_general | solution.py:139
  182.3 9.2 %fusion.40 = f32[256,256]{1,0:T(8,128)} fusion(bf16[8192,256]{1,0:T(8,128)(2,1)} %bitcast.215, bf16[169,8192]{1,0:T(8,128)(2,1)S(1)} %fusion.39, bf16[256,169]{0,1:T(8,128)(2,1)S(1)} %copy-done.18, f32[8192,256]{1,0:T(8,128)} %get-tuple-element.274), kind=kOutput, calls=%fused_computation.64 | convolution fusion | flops 1801453568 | bytes 15700480 | tf_op jit(solution)/shard_map/dot_general | solution.py:151
  191.9 39.4 %all-reduce.7.cloned.1.call-done = (f32[256,256]{1,0:T(8,128)}, f32[256,169]{0,1:T(8,128)}) async-done(((f32[256,256]{1,0:T(8,128)}, f32[256,169]{0,1:T(8,128)}), (f32[256,256]{1,0:T(8,128)}, f32[256,169]{0,1:T(8,128)})) %all-reduce.7.cloned.1.call-update) | async-done | bytes 435216 | tf_op jit(solution)/shard_map/psum | solution.py:25
  232.1 344.6 %all-reduce.5.cloned.1.call-done = (f32[256,256]{1,0:T(8,128)}, f32[256,169]{0,1:T(8,128)}) async-done(((f32[256,256]{1,0:T(8,128)}, f32[256,169]{0,1:T(8,128)}), (f32[256,256]{1,0:T(8,128)}, f32[256,169]{0,1:T(8,128)})) %all-reduce.5.cloned.1.call-update) | async-done | bytes 435216 | tf_op jit(solution)/shard_map/psum | solution.py:25
  (183 shorter events, 93.7 us)
Async XLA Ops:
  7.2 165.0 %copy-start = (bf16[256,256]{1,0:T(8,128)(2,1)S(1)}, bf16[256,256]{1,0:T(8,128)(2,1)}, u32[]{:S(2)}) copy-start(bf16[256,256]{1,0:T(8,128)(2,1)} %param.25) | copy-start | bytes 393220
  7.2 10.9 %copy-start.3 = (bf16[256,256]{1,0:T(8,128)(2,1)S(1)}, bf16[256,256]{1,0:T(8,128)(2,1)}, u32[]{:S(2)}) copy-start(bf16[256,256]{1,0:T(8,128)(2,1)} %param.16) | copy-start | bytes 393220
  7.2 10.9 %copy-start.6 = (bf16[2,256,768]{2,1,0:T(8,128)(2,1)S(1)}, bf16[2,256,768]{2,1,0:T(8,128)(2,1)}, u32[]{:S(2)}) copy-start(bf16[2,256,768]{2,1,0:T(8,128)(2,1)} %param.22) | copy-start | bytes 2359300
  7.2 11.8 %copy-start.7 = (bf16[2,256,256]{2,1,0:T(8,128)(2,1)S(1)}, bf16[2,256,256]{2,1,0:T(8,128)(2,1)}, u32[]{:S(2)}) copy-start(bf16[2,256,256]{2,1,0:T(8,128)(2,1)} %param.23) | copy-start | bytes 786436
  7.2 12.6 %copy-start.12 = (s32[8192]{0:T(1024)S(1)}, s32[8192]{0:T(1024)}, u32[]{:S(2)}) copy-start(s32[8192]{0:T(1024)} %param.19) | copy-start | bytes 98308
  7.2 12.6 %copy-start.13 = (s32[8192]{0:T(1024)S(1)}, s32[8192]{0:T(1024)}, u32[]{:S(2)}) copy-start(s32[8192]{0:T(1024)} %param.18) | copy-start | bytes 98308
  7.2 224.1 %all-reduce.7.cloned.1.call-start = ((), (), s32[]{:S(2)}) async-start(), calls=%async_computation.1 | async-start | bytes 884736 | tf_op jit(solution)/shard_map/psum | solution.py:25
  10.0 13.6 %copy-start.15 = (f32[2,256]{1,0:T(2,128)S(1)}, f32[2,256]{1,0:T(2,128)}, u32[]{:S(2)}) copy-start(f32[2,256]{1,0:T(2,128)} %param.24) | copy-start | bytes 6148
  10.1 9.8 %collective-permute-start = (bf16[1,2,64,256]{3,2,1,0:T(8,128)(2,1)S(1)}, bf16[1,2,64,256]{3,2,1,0:T(8,128)(2,1)S(1)}, u32[]{:S(2)}, u32[]{:S(2)}) collective-permute-start(bf16[1,2,64,256]{3,2,1,0:T(8,128)(2,1)S(1)} %bitcast.229), channel_id=1, source_target_pairs={{0,4},{4,8},{8,12},{12,16},{16,20},{20,24},{24,28},{28,0},{1,5},{5... | collective-permute-start | bytes 196616 | tf_op jit(solution)/shard_map/ppermute | solution.py:36
  13.3 6.6 %collective-permute-start.1 = (bf16[1,2,64,256]{3,2,1,0:T(8,128)(2,1)S(1)}, bf16[1,2,64,256]{3,2,1,0:T(8,128)(2,1)S(1)}, u32[]{:S(2)}, u32[]{:S(2)}) collective-permute-start(bf16[1,2,64,256]{3,2,1,0:T(8,128)(2,1)S(1)} %bitcast.228), channel_id=1, source_target_pairs={{4,0},{8,4},{12,8},{16,12},{20,16},{24,20},{28,24},{0,28},{5,1},{9... | collective-permute-start | bytes 196616 | tf_op jit(solution)/shard_map/ppermute | solution.py:37
  18.4 13.9 %copy-start.4 = (bf16[256,768]{1,0:T(8,128)(2,1)}, bf16[256,768]{1,0:T(8,128)(2,1)S(1)}, u32[]{:S(2)}) copy-start(bf16[256,768]{1,0:T(8,128)(2,1)S(1)} %convolution_convert_fusion.3) | copy-start | bytes 1179652
  22.1 5.0 collective-permute-start.2
  24.2 5.0 collective-permute-start.3
  38.1 6.3 %copy-start.1 = (f32[2048,512]{1,0:T(8,128)}, f32[2048,512]{1,0:T(8,128)S(1)}, u32[]{:S(2)}) copy-start(f32[2048,512]{1,0:T(8,128)S(1)} %fusion.83) | copy-start | bytes 12582916 | tf_op jit(solution)/shard_map/while
  84.5 6.3 %copy-start.1 = (f32[2048,512]{1,0:T(8,128)}, f32[2048,512]{1,0:T(8,128)S(1)}, u32[]{:S(2)}) copy-start(f32[2048,512]{1,0:T(8,128)S(1)} %fusion.83) | copy-start | bytes 12582916 | tf_op jit(solution)/shard_map/while
  97.9 7.9 %collective-permute-start.4 = (bf16[1,2,64,256]{3,2,1,0:T(8,128)(2,1)S(1)}, bf16[1,2,64,256]{3,2,1,0:T(8,128)(2,1)S(1)}, u32[]{:S(2)}, u32[]{:S(2)}) collective-permute-start(bf16[1,2,64,256]{3,2,1,0:T(8,128)(2,1)S(1)} %bitcast.231), channel_id=1, source_target_pairs={{0,4},{4,8},{8,12},{12,16},{16,20},{20,24},{24,28},{28,0},{1,5},{5... | collective-permute-start | bytes 196616 | tf_op jit(solution)/shard_map/ppermute | solution.py:36
  99.2 6.7 %collective-permute-start.5 = (bf16[1,2,64,256]{3,2,1,0:T(8,128)(2,1)S(1)}, bf16[1,2,64,256]{3,2,1,0:T(8,128)(2,1)S(1)}, u32[]{:S(2)}, u32[]{:S(2)}) collective-permute-start(bf16[1,2,64,256]{3,2,1,0:T(8,128)(2,1)S(1)} %bitcast.230), channel_id=1, source_target_pairs={{4,0},{8,4},{12,8},{16,12},{20,16},{24,20},{28,24},{0,28},{5,1},{9... | collective-permute-start | bytes 196616 | tf_op jit(solution)/shard_map/ppermute | solution.py:37
  106.0 5.0 collective-permute-start.6
  107.6 5.0 collective-permute-start.7
  117.9 6.3 %copy-start.2 = (f32[2048,512]{1,0:T(8,128)}, f32[2048,512]{1,0:T(8,128)S(1)}, u32[]{:S(2)}) copy-start(f32[2048,512]{1,0:T(8,128)S(1)} %fusion.88) | copy-start | bytes 12582916 | tf_op jit(solution)/shard_map/while
  172.2 6.9 %copy-start.17 = (bf16[169,8192]{1,0:T(8,128)(2,1)S(1)}, bf16[169,8192]{1,0:T(8,128)(2,1)}, u32[]{:S(2)}) copy-start(bf16[169,8192]{1,0:T(8,128)(2,1)} %param.27) | copy-start | bytes 8306692
  172.2 6.9 %copy-start.18 = (bf16[256,169]{0,1:T(8,128)(2,1)S(1)}, bf16[256,169]{0,1:T(8,128)(2,1)}, u32[]{:S(2)}) copy-start(bf16[256,169]{0,1:T(8,128)(2,1)} %param.26) | copy-start | bytes 259588
  182.3 49.0 %copy-start.14 = (f32[1,256]{1,0:T(1,128)S(1)}, f32[1,256]{1,0:T(1,128)}, u32[]{:S(2)}) copy-start(f32[1,256]{1,0:T(1,128)} %get-tuple-element.271) | copy-start | bytes 3076
  191.6 385.2 %all-reduce.5.cloned.1.call-start = ((), (), s32[]{:S(2)}) async-start(), calls=%async_computation | async-start | bytes 884736 | tf_op jit(solution)/shard_map/psum | solution.py:25
  (18 other events, 70.2 us)
Sparse Core Ops, SparseCore 0:
  191.7 39.5 all-reduce.6
  234.0 342.6 all-reduce.4
